TPU v7x, 128 devices: a whole 4x4x4 slice. The times are simulated.
128 devices in a mesh: seq: 16 (over x, z), head: 8 (over y, core).
Axes of the slice: x: 4, y: 4, z: 4, core: 2. Of those that a mesh axis runs over, the one named last changes fastest.
Arguments:
- queries: bfloat16 [65536, 16, 128], P(('seq', 'head'))
- keys: bfloat16 [65536, 4, 128], P('seq')
- values: bfloat16 [65536, 4, 128], P('seq')
- refine_owner: int32 [512, 4], P('seq'), may hold values from 0 to 15, all different within a row; in each aligned block of 32 rows (0 to 31, 32 to 63, ...) at most 16 rows name the same one
- refine_local: int32 [512, 4], P('seq'), may hold values from 0 to 31
Outputs:
- attended: bfloat16 [65536, 16, 128], P('seq', 'head')
Inputs may be any that keep to these rules, and one draw needn't show every extreme that they name: `refine_owner`: in each row the 4 entries differ. In the rows of one device (aligned blocks of 32 rows) no value is named more than 16 times.
All inputs are finite; a program needn't handle non-finite values.
Results may differ from a plain program's by a relative error of at most 0.008.
Values may be sent and summed in bfloat16 or wider, within the bound.
A program may use at most 128 MiB of HBM per device.

v0:
```python
import functools
import math

import jax
import jax.numpy as jnp
from jax import lax
from jax.experimental import pallas as pl
from jax.experimental.pallas import tpu as pltpu
from jax.sharding import PartitionSpec as P

MESH = pl.DeviceIdType.MESH
BLK = 128
HD = 128
KVH = 4
SIDE = 4
BLOCKS = 32
LISTED = 128
REFINE = 4
HEADS = 8
HALF = BLK // 2
MOST = 64
ROWS = 2 * BLK
MIB = 2**20
F32, BF16, I32 = jnp.float32, jnp.bfloat16, jnp.int32
DMA = pltpu.SemaphoreType.DMA


class Place:
    def __init__(self):
        self.seq, self.head = lax.axis_index("seq"), lax.axis_index("head")
        self.core = self.head % 2
        x, z = self.seq // SIDE, self.seq % SIDE
        self.a, self.b = x + self.core * (z - x), z + self.core * (x - z)
        self.stride_a, self.stride_b = SIDE - 3 * self.core, 1 + 3 * self.core
        self.sibling = (self.seq, self.head + 1 - 2 * self.core)

    def on_a(self, k):
        return (self.a + k) % SIDE

    def on_b(self, k):
        return (self.b + k) % SIDE

    def dev_a(self, k):
        return (self.on_a(k) * self.stride_a + self.b * self.stride_b, self.head)

    def dev_b(self, k):
        return (self.a * self.stride_a + self.on_b(k) * self.stride_b, self.head)

    def dev_head(self, k):
        return (self.seq, (self.head + k) % HEADS)


def remote(src, dst, send, recv, dev):
    return pltpu.make_async_remote_copy(
        src_ref=src, dst_ref=dst, send_sem=send, recv_sem=recv, device_id=dev, device_id_type=MESH
    )


def greet(peers):
    barrier = pltpu.get_barrier_semaphore()
    for dev in peers:
        pl.semaphore_signal(barrier, inc=1, device_id=dev, device_id_type=MESH)
    pl.semaphore_wait(barrier, len(peers))


def start(copies):
    for copy in copies:
        copy.start()


def spread_kernel(
    keys, values, queries, owner, local,
    rows, own, means, q_out, q_later, tabs, pos, need,
    kv_in, q_in, half, row, both, q_st, tab_out, tab_in, pos_v, need_a, need_b, mean_a, mean_b,
    in_sem, a_send, a_recv, q_send, q_recv, t_send, t_recv, n_send, n_recv, m_send, m_recv, x_send, x_recv, l_sem,
):
    at = Place()
    kv = at.head // 2
    parts = 2
    per = BLOCKS // parts
    loads = []
    for t, src in enumerate((keys, values)):
        for p in range(parts):
            where = pl.ds(p * per, per)
            loads.append(
                pltpu.make_async_copy(
                    src.at[where, pl.ds(at.core * (HALF * KVH), HALF * KVH)],
                    kv_in.at[t, where],
                    in_sem.at[t * parts + p],
                )
            )
    loads.append(pltpu.make_async_copy(queries, q_in, in_sem.at[2 * parts]))
    start(loads)

    greet(
        [at.dev_a(k) for k in range(1, SIDE)]
        + [at.dev_b(k) for k in range(1, SIDE)]
        + [at.dev_head(k) for k in range(1, HEADS)]
    )

    out_row = lax.broadcasted_iota(I32, (HALF, HALF * KVH), 0)
    in_row = lax.broadcasted_iota(I32, (HALF, HALF * KVH), 1)
    chooser = jnp.where(in_row == out_row * KVH + kv, 1.0, 0.0).astype(BF16)
    my_half = pl.ds(at.core * HALF, HALF)
    gather, to_x = [], []
    order = ((0, 1, 0), (1, 3, 2), (1, 1, 1), (0, 3, 3))
    for t in range(2):
        for p in range(parts):
            loads[t * parts + p].wait()

            @pl.loop(p * per // 4, (p + 1) * per // 4)
            def _(i, t=t):
                for u in range(4):
                    picked = jnp.dot(chooser, kv_in[t, i * 4 + u], preferred_element_type=F32)
                    picked = picked.astype(BF16)
                    half[t, i * 4 + u] = picked
                    both[t, i * 4 + u, my_half] = picked

            for part, k, n in order[:1] if p == 0 else order[1:]:
                where = pl.ds(part * per, per)
                gather.append(
                    remote(
                        half.at[t, where], row.at[t, at.a, where],
                        a_send.at[t, n], a_recv.at[t, n], at.dev_a(k),
                    )
                )
                gather[-1].start()
        to_x.append(
            remote(
                both.at[t, :, my_half], both.at[t, :, my_half],
                x_send.at[t], x_recv.at[t], at.sibling,
            )
        )
        to_x[-1].start()
    own_row = [pltpu.make_async_copy(half.at[t], row.at[t, at.a], l_sem.at[t]) for t in range(2)]
    start(own_row)

    loads[-1].wait()
    step = 16
    out_row = lax.broadcasted_iota(I32, (16 * step, 16 * step), 0)
    in_row = lax.broadcasted_iota(I32, (16 * step, 16 * step), 1)
    pair, rest = out_row // (2 * step), out_row % (2 * step)
    order = jnp.where(in_row == (rest // 2) * 16 + pair * 2 + rest % 2, 1.0, 0.0).astype(BF16)
    chunks = q_in.shape[0] // (16 * step)

    def turn(low, high):
        @pl.loop(low // 2, high // 2)
        def _(i):
            for u in range(2):
                first = pl.multiple_of((i * 2 + u) * 16 * step, 16 * step)
                turned = jnp.dot(order, q_in[pl.ds(first, 16 * step)], preferred_element_type=F32)
                turned = turned.astype(BF16)
                place = pl.multiple_of((i * 2 + u) * 2 * step, 2 * step)
                for h in range(HEADS):
                    q_st[h, pl.ds(place, 2 * step)] = turned[h * 2 * step : (h + 1) * 2 * step]

    turn(0, chunks // 2)
    now = pl.ds(0, q_st.shape[1] // 2)
    asked = [
        remote(
            q_st.at[(at.head + k) % HEADS, now], q_out.at[at.head],
            q_send.at[k - 1], q_recv.at[k - 1], at.dev_head(k),
        )
        for k in range(1, HEADS)
    ]
    start(asked)
    own_q = pltpu.make_async_copy(q_st.at[at.head, now], q_out.at[at.head], l_sem.at[2])
    own_q.start()
    turn(chunks // 2, chunks)
    later = pl.ds(q_st.shape[1] // 2, q_st.shape[1] // 2)
    later_q = pltpu.make_async_copy(q_st.at[:, later], q_later, l_sem.at[24])
    later_q.start()

    lane = lax.broadcasted_iota(I32, (LISTED, LISTED), 1)
    sub = lax.broadcasted_iota(I32, (LISTED, LISTED), 0)

    def as_row(ref):
        return jnp.concatenate([ref[r : r + 1] for r in range(REFINE)], axis=1)

    def as_column(line):
        spot = jnp.where(lane == sub, line.astype(F32), 0.0)
        return jnp.sum(spot, axis=1, keepdims=True).astype(I32)

    ow_r, lo_r = as_row(owner), as_row(local)
    ow_c, lo_c = as_column(ow_r), as_column(lo_r)
    ar, br = ow_r // SIDE, ow_r % SIDE
    ac, bc = ow_c // SIDE, ow_c % SIDE
    br, bc = br + at.core * (ar - br), bc + at.core * (ac - bc)
    ac = ac + at.core * (ow_c % SIDE - ac)
    id_r, id_c = ow_r * BLOCKS + lo_r, ow_c * BLOCKS + lo_c
    twin = id_r == id_c

    def count(mask, axis):
        ones = jnp.where(mask, 1.0, 0.0).astype(F32)
        return jnp.sum(ones, axis=axis, keepdims=True).astype(I32)

    first_r = count(twin & (sub < lane), 0) == 0
    first_c = count(twin & (lane < sub), 1) == 0
    rank_c = count((bc == br) & (lane < sub) & first_r, 1)
    pos_r = jnp.sum(jnp.where(twin & first_c, rank_c, 0), axis=0, keepdims=True)
    idx_c = ac * BLOCKS + lo_c
    for g in range(SIDE):
        wanted = first_c & (bc == g) & (rank_c == lane)
        table = jnp.sum(jnp.where(wanted, idx_c, 0), axis=0, keepdims=True)
        tab_out[g] = jnp.broadcast_to(table, (8, LISTED))
    line = lax.broadcasted_iota(I32, (8, LISTED), 0)
    pos_v[...] = jnp.where(line == 0, br * LISTED + pos_r, id_r)
    tables = [
        remote(
            tab_out.at[at.on_b(k)], tab_in.at[k], t_send.at[k - 1], t_recv.at[k - 1], at.dev_b(k)
        )
        for k in range(1, SIDE)
    ]
    start(tables)

    x_c, z_c = ow_c // SIDE, ow_c % SIDE
    x_r, z_r = ow_r // SIDE, ow_r % SIDE
    most = jnp.zeros((1, 1), F32)
    for mine_c, mine_r, here in ((x_c, x_r, at.seq // SIDE), (z_c, z_r, at.seq % SIDE)):
        rank = count((mine_c == mine_r) & (lane < sub) & first_r, 1)
        wanted = jnp.where(first_c & (mine_c != here), rank + 1, 0).astype(F32)
        most = jnp.maximum(most, jnp.max(wanted, axis=0, keepdims=True))
    need_a[at.a] = jnp.broadcast_to(most, (8, LISTED)).astype(I32)
    need_along_a = [
        remote(
            need_a.at[at.a], need_a.at[at.a], n_send.at[k - 1], n_recv.at[k - 1], at.dev_a(k)
        )
        for k in range(1, SIDE)
    ]
    start(need_along_a)
    tab_in[0] = tab_out[at.b]
    pos_copy = pltpu.make_async_copy(pos_v, pos, l_sem.at[3])
    pos_copy.start()

    passed = []
    lower, upper = pl.ds(0, per), pl.ds(per, per)
    for t in range(2):
        gather[4 * t].wait_recv()
        ref = row.at[t, at.on_a(3), lower]
        passed.append(remote(ref, ref, a_send.at[t, 4], a_recv.at[t, 4], at.dev_a(1)))
        passed[-1].start()
        gather[4 * t + 1].wait_recv()
        ref = row.at[t, at.on_a(1), upper]
        passed.append(remote(ref, ref, a_send.at[t, 5], a_recv.at[t, 5], at.dev_a(3)))
        passed[-1].start()

    take = 16
    pick_r = lax.broadcasted_iota(I32, (take, take * BLK), 0)
    pick_c = lax.broadcasted_iota(I32, (take, take * BLK), 1) // BLK
    averager = jnp.where(pick_r == pick_c, 1.0 / BLK, 0.0).astype(BF16)
    for t in range(2):
        to_x[t].wait_recv()
    for t in range(2):
        for i in range(BLOCKS // take):
            where = pl.ds(i * take, take)
            tokens = both[t, where].reshape(take * BLK, HD)
            mean = jnp.dot(averager, tokens, preferred_element_type=F32)
            mean_a[at.a, t, where] = mean.astype(BF16)
    own_out = pltpu.make_async_copy(both, own, l_sem.at[4])
    own_out.start()
    along_a = [
        remote(
            mean_a.at[at.a], mean_a.at[at.a], m_send.at[k - 1], m_recv.at[k - 1], at.dev_a(k)
        )
        for k in range(1, SIDE)
    ]
    start(along_a)
    for copy in along_a + need_along_a:
        copy.wait_recv()
    need_b[at.b] = jnp.max(need_a[...], axis=0)
    need_along_b = [
        remote(
            need_b.at[at.b], need_b.at[at.b], n_send.at[k + 2], n_recv.at[k + 2], at.dev_b(k)
        )
        for k in range(1, SIDE)
    ]
    start(need_along_b)
    for k in range(SIDE):
        mean_b[at.b, k] = mean_a[k]
    along_b = [
        remote(
            mean_b.at[at.b], mean_b.at[at.b], m_send.at[k + 2], m_recv.at[k + 2], at.dev_b(k)
        )
        for k in range(1, SIDE)
    ]
    start(along_b)
    for copy in along_b + need_along_b:
        copy.wait_recv()
    need[0, 0] = jnp.max(jnp.max(need_b[...], axis=0).astype(F32)).astype(I32)
    mean_out = [
        pltpu.make_async_copy(
            mean_b.at[n, m], means.at[m * at.stride_a + n * at.stride_b], l_sem.at[7 + n * SIDE + m]
        )
        for n in range(SIDE)
        for m in range(SIDE)
    ]
    start(mean_out)
    for copy in tables:
        copy.wait_recv()
    tab_copy = pltpu.make_async_copy(tab_in, tabs, l_sem.at[23])
    tab_copy.start()

    rows_out = []
    for t in range(2):
        gather[4 * t + 2].wait_recv()
        gather[4 * t + 3].wait_recv()
        passed[2 * t].wait_recv()
        passed[2 * t + 1].wait_recv()
        own_row[t].wait()
        rows_out.append(pltpu.make_async_copy(row.at[t], rows.at[t], l_sem.at[5 + t]))
        rows_out[-1].start()
    for copy in asked:
        copy.wait()
    for copy in rows_out + mean_out + [own_q, later_q, pos_copy, own_out, tab_copy]:
        copy.wait()
    for copy in gather + passed + to_x + tables + along_a + along_b + need_along_a + need_along_b:
        copy.wait_send()


def spread(keys, values, queries, owner, local):
    vmem, hbm = pl.BlockSpec(memory_space=pltpu.VMEM), pl.BlockSpec(memory_space=pl.ANY)
    q_rows = queries.shape[0] // HEADS
    row_shape = (2, SIDE, BLOCKS, HALF, HD)
    own_shape = (2, BLOCKS, BLK, HD)
    mean_shape = (2, BLOCKS, HD)
    return pl.pallas_call(
        spread_kernel,
        out_shape=(
            jax.ShapeDtypeStruct(row_shape, BF16),
            jax.ShapeDtypeStruct(own_shape, BF16),
            jax.ShapeDtypeStruct((SIDE * SIDE,) + mean_shape, BF16),
            jax.ShapeDtypeStruct((HEADS, q_rows // 2, HD), BF16),
            jax.ShapeDtypeStruct((HEADS, q_rows // 2, HD), BF16),
            jax.ShapeDtypeStruct((SIDE, 8, LISTED), I32),
            jax.ShapeDtypeStruct((8, LISTED), I32),
            jax.ShapeDtypeStruct((1, 1), I32),
        ),
        in_specs=[hbm, hbm, hbm, vmem, vmem],
        out_specs=(hbm,) * 7 + (pl.BlockSpec(memory_space=pltpu.SMEM),),
        scratch_shapes=[
            pltpu.VMEM((2, BLOCKS, HALF * KVH, HD), BF16),
            pltpu.VMEM(queries.shape, BF16),
            pltpu.VMEM((2, BLOCKS, HALF, HD), BF16),
            pltpu.VMEM(row_shape, BF16),
            pltpu.VMEM(own_shape, BF16),
            pltpu.VMEM((HEADS, q_rows, HD), BF16),
            pltpu.VMEM((SIDE, 8, LISTED), I32),
            pltpu.VMEM((SIDE, 8, LISTED), I32),
            pltpu.VMEM((8, LISTED), I32),
            pltpu.VMEM((SIDE, 8, LISTED), I32),
            pltpu.VMEM((SIDE, 8, LISTED), I32),
            pltpu.VMEM((SIDE,) + mean_shape, BF16),
            pltpu.VMEM((SIDE, SIDE) + mean_shape, BF16),
            DMA((5,)), DMA((2, 6)), DMA((2, 6)), DMA((HEADS - 1,)), DMA((HEADS - 1,)),
            DMA((3,)), DMA((3,)), DMA((6,)), DMA((6,)), DMA((6,)), DMA((6,)),
            DMA((2,)), DMA((2,)), DMA((25,)),
        ],
        compiler_params=pltpu.CompilerParams(
            collective_id=0, has_side_effects=True, vmem_limit_bytes=60 * MIB
        ),
        name="spread",
    )(keys, values, queries, owner, local)


def scores(left, right):
    return lax.dot_general(left, right, (((1,), (1,)), ((), ())), preferred_element_type=F32)


def pick_kernel(
    cap, tabs, pos, rows, own, means, q_first, q_later, out,
    row_k, row_v, both, mean, q, sendbuf, recv_k, recv_v, far, weights, base, q_mean, c_max, c_sum, c_val, o_st,
    in_sem, s_send, s_recv, x_send, x_recv, q_send, q_recv, o_sem,
):
    at = Place()
    row, recv = (row_k, row_v), (recv_k, recv_v)
    early, late = pl.ds(0, q.shape[1] // 2), pl.ds(q.shape[1] // 2, q.shape[1] // 2)
    loads = [pltpu.make_async_copy(rows.at[t], row[t], in_sem.at[t]) for t in range(2)]
    loads += [
        pltpu.make_async_copy(q_first, q.at[:, early], in_sem.at[2]),
        pltpu.make_async_copy(means, mean, in_sem.at[3]),
        pltpu.make_async_copy(own, both, in_sem.at[4]),
        pltpu.make_async_copy(q_later.at[at.head], q.at[at.head, late], in_sem.at[5]),
    ]
    start(loads)
    greet([at.dev_b(k) for k in range(1, SIDE)] + [at.dev_head(k) for k in range(1, HEADS)])

    picks = [[], []]
    offsets = (2, 1, 3)

    def collect(t):
        blocks = row[t].reshape(SIDE * BLOCKS, HALF, HD)
        loads[t].wait()
        for n, k in enumerate(offsets):

            @pl.loop(0, cap // 4)
            def _(i, k=k):
                for u in range(4):
                    sendbuf[t, k - 1, i * 4 + u] = blocks[tabs[k, 0, i * 4 + u]]

            picks[t].append(
                remote(
                    sendbuf.at[t, k - 1], recv[t].at[at.b, pl.ds(0, cap)],
                    s_send.at[t, n], s_recv.at[t, n], at.dev_b(-k % SIDE),
                )
            )
            if t == 0:
                picks[t][-1].start()

        @pl.loop(0, MOST // 8)
        def _(i):
            for u in range(8):
                recv[t][at.b, i * 8 + u] = blocks[tabs[0, 0, i * 8 + u]]

    collect(0)
    asked = [
        remote(
            q_later.at[(at.head + k) % HEADS], q.at[at.head, late],
            q_send.at[k - 1], q_recv.at[k - 1], at.dev_head(k),
        )
        for k in range(1, HEADS)
    ]
    start(asked)
    collect(1)

    to_log2 = math.log2(math.e)
    scale = HD**-0.5 * to_log2
    which = lax.broadcasted_iota(I32, (8, ROWS), 0)
    column = lax.broadcasted_iota(I32, (8, ROWS), 1)
    parity = jnp.where(which == column % 2, 1.0 / BLK, 0.0).astype(BF16)
    for n in (2, 3, 5):
        loads[n].wait()
    for copy in asked:
        copy.wait_recv()
    per_owner = q.shape[1] // ROWS

    def q_rows(i):
        first = pl.multiple_of((i % per_owner) * ROWS, ROWS)
        return q[i // per_owner, pl.ds(first, ROWS)]

    @pl.loop(0, BLOCKS // 4)
    def _(i):
        for u in range(4):
            q_mean[i * 4 + u] = jnp.dot(parity, q_rows(i * 4 + u), preferred_element_type=F32)

    group = 8
    total_blocks = SIDE * SIDE * BLOCKS
    key_means = mean[:, 0].reshape(total_blocks, HD)
    value_means = mean[:, 1].reshape(total_blocks, HD)

    @pl.loop(0, BLOCKS // group)
    def _(i):
        where = pl.ds(i * group, group)
        means_f = q_mean[where].reshape(group * 8, HD)
        high = means_f.astype(BF16)
        rest = means_f - high.astype(F32)
        mid = rest.astype(BF16)
        low = (rest - mid.astype(F32)).astype(BF16)
        coarse = scores(high, key_means) + scores(mid, key_means) + scores(low, key_means)
        coarse = coarse * scale + math.log2(BLK)
        number = lax.broadcasted_iota(I32, (8, total_blocks), 1)
        kept = []
        for u in range(group):
            block = i * group + u
            gone = number == at.seq * BLOCKS + block
            for r in range(REFINE):
                gone = gone | (number == pos[1, r * BLOCKS + block])
            kept.append(jnp.where(gone, 0.0, 1.0))
        kept = jnp.concatenate(kept, axis=0) > 0.0
        coarse = jnp.where(kept, coarse, -1e30)
        top = jnp.max(coarse, axis=1, keepdims=True)
        part = jnp.where(kept, jnp.exp2(coarse - top), 0.0)
        c_max[where] = jnp.broadcast_to(top, (group * 8, HD)).reshape(group, 8, HD)
        total = jnp.sum(part, axis=1, keepdims=True)
        c_sum[where] = jnp.broadcast_to(total, (group * 8, HD)).reshape(group, 8, HD)
        value = jnp.dot(part.astype(BF16), value_means, preferred_element_type=F32)
        c_val[where] = value.reshape(group, 8, HD)

    for copy in picks[0]:
        copy.wait_send()
    start(picks[1])
    loads[4].wait()

    my_half = pl.ds(at.core * HALF, HALF)
    pieces, unroll = x_send.shape[1], 4
    piece, blocks_piece = LISTED // pieces, BLOCKS // pieces

    def to_sibling(t, p):
        ref = far.at[t, pl.ds(p * piece, piece), my_half]
        return remote(ref, ref, x_send.at[t, p], x_recv.at[t, p], at.sibling)

    def line_up(t):
        for copy in picks[t]:
            copy.wait_recv()

        @pl.loop(0, pieces)
        def _(p):
            @pl.loop(0, blocks_piece // 2)
            def _(j):
                for u in range(2):
                    for r in range(REFINE):
                        i = p * blocks_piece + j * 2 + u
                        place = pos[0, r * BLOCKS + i]
                        far[t, i * REFINE + r, my_half] = recv[t][place // LISTED, place % LISTED]

            to_sibling(t, p).start()

    def fine_blocks(t, i):
        listed = far[t, pl.ds(i * REFINE, REFINE)].reshape(REFINE * BLK, HD)
        return jnp.concatenate([both[t, i], listed], axis=0)

    odd = lax.broadcasted_iota(I32, (ROWS, 1), 0) % 2 == 1

    def per_row(ref, i, width):
        return jnp.where(odd, ref[i, 1:2, :width], ref[i, 0:1, :width])

    line_up(0)

    @pl.loop(0, pieces)
    def _(p):
        to_sibling(0, p).wait_recv()

        @pl.loop(0, blocks_piece // unroll)
        def _(j):
            for u in range(unroll):
                i = p * blocks_piece + j * unroll + u
                fine = scores(q_rows(i), fine_blocks(0, i)) * scale
                coarse_top = per_row(c_max, i, 1)
                top = jnp.maximum(coarse_top, jnp.max(fine, axis=1, keepdims=True))
                fine = jnp.exp2(fine - top)
                alpha = jnp.exp2(coarse_top - top)
                total = alpha * per_row(c_sum, i, 1) + jnp.sum(fine, axis=1, keepdims=True)
                share = 1.0 / total
                weights[i] = (fine * share).astype(BF16)
                base[i] = (alpha * share) * per_row(c_val, i, HD)

    line_up(1)

    def to_out(p):
        where = pl.ds(p * blocks_piece, blocks_piece)
        return pltpu.make_async_copy(o_st.at[where], out.at[where], o_sem.at[p])

    @pl.loop(0, pieces)
    def _(p):
        to_sibling(1, p).wait_recv()

        @pl.loop(0, blocks_piece // unroll)
        def _(j):
            for u in range(unroll):
                i = p * blocks_piece + j * unroll + u
                result = jnp.dot(weights[i], fine_blocks(1, i), preferred_element_type=F32)
                o_st[i] = (result + base[i]).astype(BF16)

        to_out(p).start()

    @pl.loop(0, pieces)
    def _(p):
        to_out(p).wait()
        for t in range(2):
            to_sibling(t, p).wait_send()

    for copy in picks[1] + asked:
        copy.wait_send()


def pick(collective_id, cap, rows, own, means, q_first, q_later, tabs, pos):
    smem, hbm = pl.BlockSpec(memory_space=pltpu.SMEM), pl.BlockSpec(memory_space=pl.ANY)
    q_shape = (HEADS, 2 * q_first.shape[1], HD)
    return pl.pallas_call(
        functools.partial(pick_kernel, cap),
        out_shape=jax.ShapeDtypeStruct((BLOCKS, ROWS, HD), BF16),
        in_specs=[smem, smem, hbm, hbm, hbm, hbm, hbm],
        out_specs=hbm,
        scratch_shapes=[
            pltpu.VMEM(rows.shape[1:], BF16),
            pltpu.VMEM(rows.shape[1:], BF16),
            pltpu.VMEM(own.shape, BF16),
            pltpu.VMEM(means.shape, BF16),
            pltpu.VMEM(q_shape, BF16),
            pltpu.VMEM((2, SIDE - 1, cap, HALF, HD), BF16),
            pltpu.VMEM((SIDE, MOST, HALF, HD), BF16),
            pltpu.VMEM((SIDE, MOST, HALF, HD), BF16),
            pltpu.VMEM((2, LISTED, BLK, HD), BF16),
            pltpu.VMEM((BLOCKS, ROWS, (REFINE + 1) * BLK), BF16),
            pltpu.VMEM((BLOCKS, ROWS, HD), F32),
            pltpu.VMEM((BLOCKS, 8, HD), F32),
            pltpu.VMEM((BLOCKS, 8, HD), F32),
            pltpu.VMEM((BLOCKS, 8, HD), F32),
            pltpu.VMEM((BLOCKS, 8, HD), F32),
            pltpu.VMEM((BLOCKS, ROWS, HD), BF16),
            DMA((6,)), DMA((2, 3)), DMA((2, 3)), DMA((2, 4)), DMA((2, 4)),
            DMA((HEADS - 1,)), DMA((HEADS - 1,)), DMA((4,)),
        ],
        compiler_params=pltpu.CompilerParams(
            collective_id=collective_id, has_side_effects=True, vmem_limit_bytes=60 * MIB
        ),
        name="pick",
    )(tabs, pos, rows, own, means, q_first, q_later)


def hand_on_kernel(src, dst, held, in_sem, out_sem):
    parts = in_sem.shape[0]
    per = BLOCKS // parts
    where = [pl.ds(p * per, per) for p in range(parts)]
    inward = [
        pltpu.make_async_copy(src.at[w], held.at[w], in_sem.at[p]) for p, w in enumerate(where)
    ]
    outward = [
        pltpu.make_async_copy(held.at[w], dst.at[w], out_sem.at[p]) for p, w in enumerate(where)
    ]
    start(inward)
    for before, after in zip(inward, outward):
        before.wait()
        after.start()
    for copy in outward:
        copy.wait()


def hand_on(result):
    hbm = pl.BlockSpec(memory_space=pl.ANY)
    return pl.pallas_call(
        hand_on_kernel,
        out_shape=jax.ShapeDtypeStruct(result.shape, result.dtype),
        in_specs=[hbm],
        out_specs=hbm,
        scratch_shapes=[pltpu.VMEM(result.shape, result.dtype), DMA((8,)), DMA((8,))],
        compiler_params=pltpu.CompilerParams(vmem_limit_bytes=60 * MIB),
        name="hand_on",
    )(result)


def blank():
    def kernel(out):
        del out

    return pl.pallas_call(
        kernel,
        out_shape=jax.ShapeDtypeStruct((BLOCKS, ROWS, HD), BF16),
        out_specs=pl.BlockSpec(memory_space=pl.ANY),
        name="blank",
    )()


def on_device(queries, keys, values, refine_owner, refine_local):
    *moved, need = spread(
        keys.reshape(BLOCKS, BLK * KVH, HD),
        values.reshape(BLOCKS, BLK * KVH, HD),
        queries.reshape(-1, HD),
        refine_owner.T,
        refine_local.T,
    )
    caps = (40, 44, 52, MOST)
    most = need[0, 0]
    level = sum((most > cap).astype(I32) for cap in caps[:-1])

    def branch(n):
        return lambda *operands: hand_on(pick(n + 1, caps[n], *operands))

    out = blank()
    for n in range(len(caps)):
        run = branch(n)
        out = lax.fori_loop(0, (level == n).astype(I32), lambda _, kept: run(*moved), out)
    return out.reshape(BLOCKS * BLK, 2, HD)


def solution(mesh):
    return jax.shard_map(
        on_device,
        mesh=mesh,
        in_specs=(
            P(("seq", "head"), None, None),
            P("seq", None, None),
            P("seq", None, None),
            P("seq", None),
            P("seq", None),
        ),
        out_specs=P("seq", "head", None),
        check_vma=False,
    )
```

profile of v0, /device:TPU:1, one launch (start us, length us, event | category | flops | bytes accessed | tf_op | source)
XLA Modules:
  0.0 89.4 jit_solution(256161013484895561)
XLA Ops:
  0.0 37.2 %spread.1 = (bf16[2,4,32,64,128]{4,3,2,1,0:T(8,128)(2,1)}, bf16[2,32,128,128]{3,2,1,0:T(8,128)(2,1)S(1)}, bf16[16,2,32,128]{3,2,1,0:T(8,128)(2,1)S(1)}, bf16[8,5...) custom-call(bf16[32,512,128]{2,1,0:T(8,128)(2,1)} %bitcast.10, ...), custom_call_target="tpu_custom_call" | custom-call | tf_op jit(solution)/shard_map/spread/pallas_call | solution.py:326
  39.3 49.8 %while.41 = (s32[]{:T(128)}, bf16[32,256,128]{2,1,0:T(8,128)(2,1)}, s32[]{:T(128)}, s32[4,8,128]{2,1,0:T(8,128)S(1)}, s32[8,128]{1,0:T(8,128)S(1)}, /*index=5*/b...) while((s32[]{:T(128)}, bf16[32,256,128]{2,1,0:T(8,128)(2,1)}, ...), condition=%wide.region_3.0_spmd, body=%wide.region_2.0_spmd.sunk | while | flops 2 | bytes 109 | solution.py:661
  39.3 47.3 %pick.5.src = bf16[32,256,128]{2,1,0:T(8,128)(2,1)} custom-call(s32[4,8,128]{2,1,0:T(8,128)S(1)} %get-tuple-element.611.tabs, s32[8,128]{1,0:T(8,128)S(1)} %get-tuple-element.612.pos, bf16[2,4,32,64,128]{4,3,2,1,0:T(8,128)(2,1)} %get-tuple-element.613.rows, bf16[2,32,128,128]{3,2,1,0:T(8,128)(2,1)S(1)} %get-tuple-element.614.own, ...), custom_call_target="tpu_custom_call" | custom-call | tf_op jit(solution)/shard_map/while/body/pick/pallas_call | solution.py:568
  86.6 2.4 %hand_on.5 = bf16[32,256,128]{2,1,0:T(8,128)(2,1)} custom-call(bf16[32,256,128]{2,1,0:T(8,128)(2,1)} %pick.5.src), custom_call_target="tpu_custom_call" | custom-call | tf_op jit(solution)/shard_map/while/body/hand_on/pallas_call | solution.py:620
  89.1 0.2 while.42
  (3 shorter events, 0.0 us)
where the time goes:
time: 89.6 us; the launch traced here: 89.4 us
  Pallas kernels  86.9 us (97%)
  between operations  2.26 us (3%)
    pallas_call x1, Pallas kernels, pick(): pl.pallas_call(functools.partial(pick_kernel, cap), out_shape=jax.ShapeDt...  47.3 us
    pallas_call x1, Pallas kernels, spread(): pl.pallas_call(spread_kernel, out_shape=(jax.ShapeDtypeStruct(row_shape,...  37.2 us
    pallas_call x1, Pallas kernels, hand_on(): pl.pallas_call(hand_on_kernel, out_shape=jax.ShapeDtypeStruct(result.shap...  2.39 us

commit v1 on v0

--- a/solution.py
+++ b/solution.py
@@ -60,7 +60,10 @@
     barrier = pltpu.get_barrier_semaphore()
     for dev in peers:
         pl.semaphore_signal(barrier, inc=1, device_id=dev, device_id_type=MESH)
-    pl.semaphore_wait(barrier, len(peers))
+
+
+def wait_greeted(peers):
+    pl.semaphore_wait(pltpu.get_barrier_semaphore(), len(peers))
 
 
 def start(copies):
@@ -71,7 +74,7 @@
 def spread_kernel(
     keys, values, queries, owner, local,
     rows, own, means, q_out, q_later, tabs, pos, need,
-    kv_in, q_in, half, row, both, q_st, tab_out, tab_in, pos_v, need_a, need_b, mean_a, mean_b,
+    kv_in, q_in, half, both, q_st, tab_out, tab_in, pos_v, need_a, need_b, mean_a, mean_b,
     in_sem, a_send, a_recv, q_send, q_recv, t_send, t_recv, n_send, n_recv, m_send, m_recv, x_send, x_recv, l_sem,
 ):
     at = Place()
@@ -91,12 +94,10 @@
             )
     loads.append(pltpu.make_async_copy(queries, q_in, in_sem.at[2 * parts]))
     start(loads)
-
-    greet(
-        [at.dev_a(k) for k in range(1, SIDE)]
-        + [at.dev_b(k) for k in range(1, SIDE)]
-        + [at.dev_head(k) for k in range(1, HEADS)]
-    )
+    peers = [at.dev_a(k) for k in range(1, SIDE)]
+    peers += [at.dev_b(k) for k in range(1, SIDE)]
+    peers += [at.dev_head(k) for k in range(1, HEADS)]
+    greet(peers)
 
     out_row = lax.broadcasted_iota(I32, (HALF, HALF * KVH), 0)
     in_row = lax.broadcasted_iota(I32, (HALF, HALF * KVH), 1)
@@ -116,11 +117,13 @@
                     half[t, i * 4 + u] = picked
                     both[t, i * 4 + u, my_half] = picked
 
+            if t + p == 0:
+                wait_greeted(peers)
             for part, k, n in order[:1] if p == 0 else order[1:]:
                 where = pl.ds(part * per, per)
                 gather.append(
                     remote(
-                        half.at[t, where], row.at[t, at.a, where],
+                        half.at[t, where], rows.at[t, at.a, where],
                         a_send.at[t, n], a_recv.at[t, n], at.dev_a(k),
                     )
                 )
@@ -132,7 +135,7 @@
             )
         )
         to_x[-1].start()
-    own_row = [pltpu.make_async_copy(half.at[t], row.at[t, at.a], l_sem.at[t]) for t in range(2)]
+    own_row = [pltpu.make_async_copy(half.at[t], rows.at[t, at.a], l_sem.at[t]) for t in range(2)]
     start(own_row)
 
     loads[-1].wait()
@@ -166,6 +169,20 @@
     start(asked)
     own_q = pltpu.make_async_copy(q_st.at[at.head, now], q_out.at[at.head], l_sem.at[2])
     own_q.start()
+    passed = []
+    lower, upper = pl.ds(0, per), pl.ds(per, per)
+
+    def forward(t):
+        gather[4 * t].wait_recv()
+        ref = rows.at[t, at.on_a(3), lower]
+        passed.append(remote(ref, ref, a_send.at[t, 4], a_recv.at[t, 4], at.dev_a(1)))
+        passed[-1].start()
+        gather[4 * t + 1].wait_recv()
+        ref = rows.at[t, at.on_a(1), upper]
+        passed.append(remote(ref, ref, a_send.at[t, 5], a_recv.at[t, 5], at.dev_a(3)))
+        passed[-1].start()
+
+    forward(0)
     turn(chunks // 2, chunks)
     later = pl.ds(q_st.shape[1] // 2, q_st.shape[1] // 2)
     later_q = pltpu.make_async_copy(q_st.at[:, later], q_later, l_sem.at[24])
@@ -183,10 +200,8 @@
 
     ow_r, lo_r = as_row(owner), as_row(local)
     ow_c, lo_c = as_column(ow_r), as_column(lo_r)
-    ar, br = ow_r // SIDE, ow_r % SIDE
-    ac, bc = ow_c // SIDE, ow_c % SIDE
-    br, bc = br + at.core * (ar - br), bc + at.core * (ac - bc)
-    ac = ac + at.core * (ow_c % SIDE - ac)
+    x_r, z_r = ow_r // SIDE, ow_r % SIDE
+    x_c, z_c = ow_c // SIDE, ow_c % SIDE
     id_r, id_c = ow_r * BLOCKS + lo_r, ow_c * BLOCKS + lo_c
     twin = id_r == id_c
 
@@ -196,15 +211,22 @@
 
     first_r = count(twin & (sub < lane), 0) == 0
     first_c = count(twin & (lane < sub), 1) == 0
-    rank_c = count((bc == br) & (lane < sub) & first_r, 1)
-    pos_r = jnp.sum(jnp.where(twin & first_c, rank_c, 0), axis=0, keepdims=True)
+    rank_z = count((z_c == z_r) & (lane < sub) & first_r, 1)
+    rank_x = count((x_c == x_r) & (lane < sub) & first_r, 1)
+    places = [
+        group * LISTED
+        + jnp.sum(jnp.where(twin & first_c, rank, 0), axis=0, keepdims=True)
+        for group, rank in ((z_r, rank_z), (x_r, rank_x))
+    ]
+    rank_c = rank_z + at.core * (rank_x - rank_z)
+    ac, bc = x_c + at.core * (z_c - x_c), z_c + at.core * (x_c - z_c)
     idx_c = ac * BLOCKS + lo_c
     for g in range(SIDE):
         wanted = first_c & (bc == g) & (rank_c == lane)
         table = jnp.sum(jnp.where(wanted, idx_c, 0), axis=0, keepdims=True)
         tab_out[g] = jnp.broadcast_to(table, (8, LISTED))
     line = lax.broadcasted_iota(I32, (8, LISTED), 0)
-    pos_v[...] = jnp.where(line == 0, br * LISTED + pos_r, id_r)
+    pos_v[...] = jnp.where(line == 0, places[0], jnp.where(line == 1, places[1], id_r))
     tables = [
         remote(
             tab_out.at[at.on_b(k)], tab_in.at[k], t_send.at[k - 1], t_recv.at[k - 1], at.dev_b(k)
@@ -213,12 +235,9 @@
     ]
     start(tables)
 
-    x_c, z_c = ow_c // SIDE, ow_c % SIDE
-    x_r, z_r = ow_r // SIDE, ow_r % SIDE
     most = jnp.zeros((1, 1), F32)
-    for mine_c, mine_r, here in ((x_c, x_r, at.seq // SIDE), (z_c, z_r, at.seq % SIDE)):
-        rank = count((mine_c == mine_r) & (lane < sub) & first_r, 1)
-        wanted = jnp.where(first_c & (mine_c != here), rank + 1, 0).astype(F32)
+    for group, rank, here in ((x_c, rank_x, at.seq // SIDE), (z_c, rank_z, at.seq % SIDE)):
+        wanted = jnp.where(first_c & (group != here), rank + 1, 0).astype(F32)
         most = jnp.maximum(most, jnp.max(wanted, axis=0, keepdims=True))
     need_a[at.a] = jnp.broadcast_to(most, (8, LISTED)).astype(I32)
     need_along_a = [
@@ -232,17 +251,7 @@
     pos_copy = pltpu.make_async_copy(pos_v, pos, l_sem.at[3])
     pos_copy.start()
 
-    passed = []
-    lower, upper = pl.ds(0, per), pl.ds(per, per)
-    for t in range(2):
-        gather[4 * t].wait_recv()
-        ref = row.at[t, at.on_a(3), lower]
-        passed.append(remote(ref, ref, a_send.at[t, 4], a_recv.at[t, 4], at.dev_a(1)))
-        passed[-1].start()
-        gather[4 * t + 1].wait_recv()
-        ref = row.at[t, at.on_a(1), upper]
-        passed.append(remote(ref, ref, a_send.at[t, 5], a_recv.at[t, 5], at.dev_a(3)))
-        passed[-1].start()
+    forward(1)
 
     take = 16
     pick_r = lax.broadcasted_iota(I32, (take, take * BLK), 0)
@@ -300,18 +309,14 @@
     tab_copy = pltpu.make_async_copy(tab_in, tabs, l_sem.at[23])
     tab_copy.start()
 
-    rows_out = []
     for t in range(2):
         gather[4 * t + 2].wait_recv()
         gather[4 * t + 3].wait_recv()
         passed[2 * t].wait_recv()
         passed[2 * t + 1].wait_recv()
-        own_row[t].wait()
-        rows_out.append(pltpu.make_async_copy(row.at[t], rows.at[t], l_sem.at[5 + t]))
-        rows_out[-1].start()
     for copy in asked:
         copy.wait()
-    for copy in rows_out + mean_out + [own_q, later_q, pos_copy, own_out, tab_copy]:
+    for copy in own_row + mean_out + [own_q, later_q, pos_copy, own_out, tab_copy]:
         copy.wait()
     for copy in gather + passed + to_x + tables + along_a + along_b + need_along_a + need_along_b:
         copy.wait_send()
@@ -341,7 +346,6 @@
             pltpu.VMEM((2, BLOCKS, HALF * KVH, HD), BF16),
             pltpu.VMEM(queries.shape, BF16),
             pltpu.VMEM((2, BLOCKS, HALF, HD), BF16),
-            pltpu.VMEM(row_shape, BF16),
             pltpu.VMEM(own_shape, BF16),
             pltpu.VMEM((HEADS, q_rows, HD), BF16),
             pltpu.VMEM((SIDE, 8, LISTED), I32),
@@ -382,7 +386,9 @@
         pltpu.make_async_copy(q_later.at[at.head], q.at[at.head, late], in_sem.at[5]),
     ]
     start(loads)
-    greet([at.dev_b(k) for k in range(1, SIDE)] + [at.dev_head(k) for k in range(1, HEADS)])
+    peers = [at.dev_b(k) for k in range(1, SIDE)] + [at.dev_head(k) for k in range(1, HEADS)]
+    greet(peers)
+    wait_greeted(peers)
 
     picks = [[], []]
     offsets = (2, 1, 3)
@@ -463,7 +469,7 @@
             block = i * group + u
             gone = number == at.seq * BLOCKS + block
             for r in range(REFINE):
-                gone = gone | (number == pos[1, r * BLOCKS + block])
+                gone = gone | (number == pos[2, r * BLOCKS + block])
             kept.append(jnp.where(gone, 0.0, 1.0))
         kept = jnp.concatenate(kept, axis=0) > 0.0
         coarse = jnp.where(kept, coarse, -1e30)
@@ -475,9 +481,9 @@
         value = jnp.dot(part.astype(BF16), value_means, preferred_element_type=F32)
         c_val[where] = value.reshape(group, 8, HD)
 
-    for copy in picks[0]:
-        copy.wait_send()
-    start(picks[1])
+    for before, after in zip(*picks):
+        before.wait_send()
+        after.start()
     loads[4].wait()
 
     my_half = pl.ds(at.core * HALF, HALF)
@@ -499,7 +505,7 @@
                 for u in range(2):
                     for r in range(REFINE):
                         i = p * blocks_piece + j * 2 + u
-                        place = pos[0, r * BLOCKS + i]
+                        place = pos[at.core, r * BLOCKS + i]
                         far[t, i * REFINE + r, my_half] = recv[t][place // LISTED, place % LISTED]
 
             to_sibling(t, p).start()
@@ -519,10 +525,10 @@
     def _(p):
         to_sibling(0, p).wait_recv()
 
-        @pl.loop(0, blocks_piece // unroll)
+        @pl.loop(0, blocks_piece // 8)
         def _(j):
-            for u in range(unroll):
-                i = p * blocks_piece + j * unroll + u
+            for u in range(8):
+                i = p * blocks_piece + j * 8 + u
                 fine = scores(q_rows(i), fine_blocks(0, i)) * scale
                 coarse_top = per_row(c_max, i, 1)
                 top = jnp.maximum(coarse_top, jnp.max(fine, axis=1, keepdims=True))
@@ -591,7 +597,7 @@
             DMA((HEADS - 1,)), DMA((HEADS - 1,)), DMA((4,)),
         ],
         compiler_params=pltpu.CompilerParams(
-            collective_id=collective_id, has_side_effects=True, vmem_limit_bytes=60 * MIB
+            collective_id=collective_id, has_side_effects=True, vmem_limit_bytes=50 * MIB
         ),
         name="pick",
     )(tabs, pos, rows, own, means, q_first, q_later)
@@ -623,7 +629,7 @@
         in_specs=[hbm],
         out_specs=hbm,
         scratch_shapes=[pltpu.VMEM(result.shape, result.dtype), DMA((8,)), DMA((8,))],
-        compiler_params=pltpu.CompilerParams(vmem_limit_bytes=60 * MIB),
+        compiler_params=pltpu.CompilerParams(vmem_limit_bytes=24 * MIB),
         name="hand_on",
     )(result)
 

time: 89.6 us -> 84.9 us (0.948)
  Pallas kernels: 86.9 us -> 82.1 us
    pallas_call x1, Pallas kernels: 37.2 us -> 34.6 us  [spread(): pl.pallas_call(spread_kernel, out_shape=(jax.ShapeDtypeStruct(row_shape,...]
    pallas_call x1, Pallas kernels: 47.3 us -> 46 us  [pick(): pl.pallas_call(functools.partial(pick_kernel, cap), out_shape=jax.ShapeDt...]
where the time goes in v1:
time: 84.9 us; the launch traced here: 84.7 us
  Pallas kernels  82.1 us (97%)
  between operations  2.1 us (2%)
    pallas_call x1, Pallas kernels, pick(): pl.pallas_call(functools.partial(pick_kernel, cap), out_shape=jax.ShapeDt...  46 us
    pallas_call x1, Pallas kernels, spread(): pl.pallas_call(spread_kernel, out_shape=(jax.ShapeDtypeStruct(row_shape,...  34.6 us

profile of v1, /device:TPU:1, one launch (start us, length us, event | category | flops | bytes accessed | tf_op | source)
XLA Modules:
  0.0 84.7 jit_solution(4442389153228735972)
XLA Ops:
  0.0 34.6 %spread.1 = (bf16[2,4,32,64,128]{4,3,2,1,0:T(8,128)(2,1)}, bf16[2,32,128,128]{3,2,1,0:T(8,128)(2,1)S(1)}, bf16[16,2,32,128]{3,2,1,0:T(8,128)(2,1)S(1)}, bf16[8,5...) custom-call(bf16[32,512,128]{2,1,0:T(8,128)(2,1)} %bitcast.10, ...), custom_call_target="tpu_custom_call" | custom-call | tf_op jit(solution)/shard_map/spread/pallas_call | solution.py:331
  36.5 47.8 %while.41 = (s32[]{:T(128)}, bf16[32,256,128]{2,1,0:T(8,128)(2,1)}, s32[]{:T(128)}, s32[4,8,128]{2,1,0:T(8,128)S(1)}, s32[8,128]{1,0:T(8,128)S(1)}, /*index=5*/b...) while((s32[]{:T(128)}, bf16[32,256,128]{2,1,0:T(8,128)(2,1)}, ...), condition=%wide.region_3.0_spmd, body=%wide.region_2.0_spmd.sunk | while | flops 2 | bytes 109 | solution.py:667
  36.7 46.0 %pick.5.src = bf16[32,256,128]{2,1,0:T(8,128)(2,1)S(1)} custom-call(s32[4,8,128]{2,1,0:T(8,128)S(1)} %get-tuple-element.611.tabs, s32[8,128]{1,0:T(8,128)S(1)} %get-tuple-element.612.pos, bf16[2,4,32,64,128]{4,3,2,1,0:T(8,128)(2,1)} %get-tuple-element.613.rows, bf16[2,32,128,128]{3,2,1,0:T(8,128)(2,1)S(1)} %get-tuple-element.614.own, ...), custom_call_target="tpu_custom_call" | custom-call | tf_op jit(solution)/shard_map/while/body/pick/pallas_call | solution.py:574
  82.6 1.6 %hand_on.5 = bf16[32,256,128]{2,1,0:T(8,128)(2,1)} custom-call(bf16[32,256,128]{2,1,0:T(8,128)(2,1)S(1)} %pick.5.src), custom_call_target="tpu_custom_call" | custom-call | tf_op jit(solution)/shard_map/while/body/hand_on/pallas_call | solution.py:626
  84.3 0.2 while.43
  (3 shorter events, 0.0 us)
